TPU v7x, 512 devices: a whole 4x8x8 slice. The times are simulated.
512 devices in a mesh: sea: 32 (over y, x_lo, core), fault: 16 (over z, x_hi).
Axes of the slice: x: 4 (x_hi: 2, x_lo: 2; x = x_hi * 2 + x_lo), y: 8, z: 8, core: 2. Of those that a mesh axis runs over, the one named last changes fastest.
Arguments:
- slip_rate: bfloat16 [65536, 128], P(('fault', 'sea')), may hold values from -6 to 6
- near_blocks: bfloat16 [32, 16, 8, 256, 256], P('sea', 'fault'), may hold values from -0.375 to 0.375
- near_rows: int32 [32, 16, 8], P('sea', 'fault'), may hold values from 0 to 15
- near_cols: int32 [32, 16, 8], P('sea', 'fault'), may hold values from 0 to 15
- near_scale: float32 [32, 16, 8], P('sea', 'fault'), may hold values from 0.1 to 0.5
- far_left: bfloat16 [32, 16, 24, 48, 256], P('sea', 'fault'), may hold values from -0.875 to 0.875
- far_right: bfloat16 [32, 16, 24, 48, 256], P('sea', 'fault'), may hold values from -0.375 to 0.375
- far_rows: int32 [32, 16, 24], P('sea', 'fault'), may hold values from 0 to 15
- far_cols: int32 [32, 16, 24], P('sea', 'fault'), may hold values from 0 to 15
- far_rank: int32 [32, 16, 24], P('sea', 'fault'), may hold values from 16 to 48, as said below
- far_scale: float32 [32, 16, 24], P('sea', 'fault'), may hold values from 0.1 to 0.5
- sea_depth: float32 [512, 256], P('sea', 'fault'), may hold values from 0.3 to 1
- wet_mask: int32 [512, 256], P('sea', 'fault'), may hold values 0 or 1
Outputs:
- uplift: float32 [512, 256, 128], P('sea', 'fault')
- sea_level: float32 [512, 256, 128], P('sea', 'fault')
Inputs may be any that keep to these rules, and one draw needn't show every extreme that they name: `far_rank`: block 0 of every device has rank 48; every rank is at least 16.
All inputs are finite; a program needn't handle non-finite values. No bound on the sum of `wet_mask` on one device may be relied on, other than what follows from the above.
Results may differ from a plain program's by a relative error of at most 0.0024.
Values may be sent and summed in bfloat16 or wider, within the bound.
A program may use at most 64 MiB of HBM per device.

v0:
```python
import jax
import jax.numpy as jnp
from jax import lax
from jax.sharding import PartitionSpec as P

STEPS = 6
gravity_step = 0.7
height_step = 0.7


def extended(cells, sides, width):
    for axis, dim in sides:
        count = lax.axis_size(axis)
        ends = count - 1
        head = lax.slice_in_dim(cells, 0, width, axis=dim)
        tail = lax.slice_in_dim(cells, cells.shape[dim] - width, cells.shape[dim], axis=dim)
        cells = jnp.concatenate(
            [
                lax.ppermute(tail, axis, [(i, (i + 1) % count) for i in range(ends)]),
                cells,
                lax.ppermute(head, axis, [((i + 1) % count, i) for i in range(ends)]),
            ],
            axis=dim,
        )
    return cells


def advance(height, east_flow, north_flow, depth_pad):
    new_east = east_flow[1:-1, :-1] - gravity_step * (height[1:-1, 1:] - height[1:-1, :-1])
    east_depth = jnp.minimum(depth_pad[1:-1, :-1], depth_pad[1:-1, 1:])
    flux_east = east_depth[:, :, None] * new_east
    new_north = north_flow[:-1, 1:-1] - gravity_step * (height[1:, 1:-1] - height[:-1, 1:-1])
    north_depth = jnp.minimum(depth_pad[:-1, 1:-1], depth_pad[1:, 1:-1])
    flux_north = north_depth[:, :, None] * new_north
    change = flux_east[:, 1:] - flux_east[:, :-1] + flux_north[1:] - flux_north[:-1]
    new_height = height[1:-1, 1:-1] - height_step * change
    return (new_height, new_east[:, 1:], new_north[1:])


def on_device(
    slip_rate,
    near_blocks,
    near_rows,
    near_cols,
    near_scale,
    far_left,
    far_right,
    far_rows,
    far_cols,
    far_rank,
    far_scale,
    sea_depth,
    wet_mask,
):
    brick_y, brick_x = sea_depth.shape
    fault_count = lax.axis_size("fault")
    leaf_size = near_blocks.shape[-1]
    rank_pad = far_left.shape[-2]
    members = slip_rate.shape[1]
    leaf_count = brick_y * brick_x * fault_count // leaf_size
    targets = jnp.arange(leaf_count)
    gathered = lax.all_gather(slip_rate, "sea", axis=0, tiled=True)
    leaves = gathered.reshape(-1, leaf_size, members)
    near_slip = leaves[near_cols[0, 0]]
    near_term = jnp.einsum(
        "bij,bjs->bis", near_blocks[0, 0], near_slip, preferred_element_type=jnp.float32
    )
    near_weight = (near_rows[0, 0][:, None] == targets).astype(jnp.float32) * near_scale[0, 0][
        :, None
    ]
    total = jnp.einsum("br,bis->ris", near_weight, near_term, precision=lax.Precision.HIGHEST)
    far_slip = leaves[far_cols[0, 0]]
    coeffs = jnp.einsum(
        "bkc,bcs->bks", far_right[0, 0], far_slip, preferred_element_type=jnp.float32
    )
    kept = jnp.arange(rank_pad)[None, :, None] < far_rank[0, 0][:, None, None]
    coeffs = jnp.where(kept, coeffs, jnp.float32(0.0)).astype(jnp.bfloat16)
    far_term = jnp.einsum(
        "bki,bks->bis", far_left[0, 0], coeffs, preferred_element_type=jnp.float32
    )
    far_weight = (far_rows[0, 0][:, None] == targets).astype(jnp.float32) * far_scale[0, 0][:, None]
    total = total + jnp.einsum("br,bis->ris", far_weight, far_term, precision=lax.Precision.HIGHEST)
    partial_value = total.reshape(brick_y, fault_count, brick_x, members)
    ordered = jnp.transpose(partial_value, (1, 0, 2, 3))
    summed = lax.psum_scatter(ordered, "fault", scatter_dimension=0, tiled=True)
    uplift = summed[0]
    wet = wet_mask.astype(jnp.float32)
    depth_cell = sea_depth * wet
    height = uplift * wet[:, :, None]
    east_flow = jnp.zeros_like(height)
    north_flow = jnp.zeros_like(height)
    depth_pad = extended(depth_cell, (("sea", 0), ("fault", 1)), 1)
    for step_index in range(STEPS):
        padded = (
            extended(height, (("sea", 0), ("fault", 1)), 1),
            extended(east_flow, (("sea", 0), ("fault", 1)), 1),
            extended(north_flow, (("sea", 0), ("fault", 1)), 1),
        )
        height, east_flow, north_flow = advance(padded[0], padded[1], padded[2], depth_pad)
    return (uplift, height)


def solution(mesh):
    placed = (
        P(("fault", "sea"), None),
        P("sea", "fault", None, None, None),
        P("sea", "fault", None),
        P("sea", "fault", None),
        P("sea", "fault", None),
        P("sea", "fault", None, None, None),
        P("sea", "fault", None, None, None),
        P("sea", "fault", None),
        P("sea", "fault", None),
        P("sea", "fault", None),
        P("sea", "fault", None),
        P("sea", "fault"),
        P("sea", "fault"),
    )
    return jax.shard_map(
        on_device,
        mesh=mesh,
        in_specs=placed,
        out_specs=(P("sea", "fault", None), P("sea", "fault", None)),
        check_vma=False,
    )
```

profile of v0, /device:TPU:288, one launch (start us, length us, event | category | flops | bytes accessed | tf_op | source)
XLA Modules:
  0.0 510.8 jit_solution(5362446358330737596)
XLA Ops:
  10.0 66.4 %all-gather.2.cloned.1.call-done = bf16[4096,128]{1,0:T(8,128)(2,1)} async-done(((bf16[128,128]{1,0:T(8,128)(2,1)}), bf16[4096,128]{1,0:T(8,128)(2,1)}) %all-gather.2.cloned.1.call-update) | async-done | bytes 1048592 | tf_op jit(solution)/shard_map/all_gather | solution.py:62
  76.4 2.1 gather_fusion.1
  78.5 3.8 fusion.5
  82.3 3.6 copy.17
  91.3 2.0 fusion.2
  93.3 2.0 copy.19
  95.3 2.1 collective-permute-start.4
  97.4 5.5 %collective-permute-start.5 = (f32[1,16,128]{2,1,0:T(8,128)S(1)}, f32[1,16,128]{2,1,0:T(8,128)S(1)}, u32[]{:S(2)}, u32[]{:S(2)}) collective-permute-start(f32[1,16,128]{2,1,0:T(8,128)S(1)} %broadcast.92), channel_id=1, source_target_pairs={{16,0},{32,16},{48,32},{64,48},{80,64},{96,80},{112,96},{128,112},... | collective-permute-start | bytes 24584 | tf_op jit(solution)/shard_map/ppermute | solution.py:21
  103.0 1.9 collective-permute-start
  105.0 5.8 %collective-permute-start.1 = (f32[1,16]{1,0:T(1,128)S(1)}, f32[1,16]{1,0:T(1,128)S(1)}, u32[]{:S(2)}, u32[]{:S(2)}) collective-permute-start(f32[1,16]{1,0:T(1,128)S(1)} %get-tuple-element.58), channel_id=1, source_target_pairs={{16,0},{32,16},{48,32},{64,48},{80,64},{96,80},{112,96},{128,112},... | collective-permute-start | bytes 200 | tf_op jit(solution)/shard_map/ppermute | solution.py:21
  112.1 4.9 collective-permute-start.2
  117.0 4.6 collective-permute-start.3
  121.6 2.5 collective-permute-done.3
  124.1 184.5 %reduce-scatter.2.cloned.1.call-done = f32[1,16,16,128]{3,2,1,0:T(8,128)} async-done(((f32[16,16,16,128]{3,2,1,0:T(8,128)}), f32[1,16,16,128]{3,2,1,0:T(8,128)}) %reduce-scatter.2.cloned.1.call-update) | async-done | bytes 131088 | tf_op jit(solution)/shard_map/reduce_scatter | solution.py:85
  309.7 1.9 collective-permute-start.7
  311.6 5.8 %collective-permute-start.8 = (f32[1,16,128]{2,1,0:T(8,128)S(1)}, f32[1,16,128]{2,1,0:T(8,128)S(1)}, u32[]{:S(2)}, u32[]{:S(2)}) collective-permute-start(f32[1,16,128]{2,1,0:T(8,128)S(1)} %get-tuple-element.54), channel_id=1, source_target_pairs={{16,0},{32,16},{48,32},{64,48},{80,64},{96,80},{112,96},{128,112},... | collective-permute-start | bytes 24584 | tf_op jit(solution)/shard_map/ppermute | solution.py:21
  317.4 2.5 collective-permute-start.6
  319.9 3.9 collective-permute-start.10
  323.8 5.6 %collective-permute-start.9 = (f32[18,1,128]{2,1,0:T(1,128)S(1)}, f32[18,1,128]{2,1,0:T(1,128)S(1)}, u32[]{:S(2)}, u32[]{:S(2)}) collective-permute-start(f32[18,1,128]{2,1,0:T(1,128)S(1)} %get-tuple-element.42), channel_id=1, source_target_pairs={{1,0},{2,1},{3,2},{4,3},{5,4},{6,5},{7,6},{8,7},{9,8},{10,9},{11,1... | collective-permute-start | bytes 27656 | tf_op jit(solution)/shard_map/ppermute | solution.py:21
  329.5 1.9 collective-permute-start.18
  331.6 1.9 collective-permute-start.11
  333.6 5.8 %collective-permute-start.12 = (f32[1,16,128]{2,1,0:T(8,128)S(1)}, f32[1,16,128]{2,1,0:T(8,128)S(1)}, u32[]{:S(2)}, u32[]{:S(2)}) collective-permute-start(f32[1,16,128]{2,1,0:T(8,128)S(1)} %get-tuple-element.31), channel_id=1, source_target_pairs={{16,0},{32,16},{48,32},{64,48},{80,64},{96,80},{112,96},{128,112},... | collective-permute-start | bytes 24584 | tf_op jit(solution)/shard_map/ppermute | solution.py:21
  339.5 1.9 collective-permute-start.14
  341.4 5.8 %collective-permute-start.15 = (f32[1,16,128]{2,1,0:T(8,128)S(1)}, f32[1,16,128]{2,1,0:T(8,128)S(1)}, u32[]{:S(2)}, u32[]{:S(2)}) collective-permute-start(f32[1,16,128]{2,1,0:T(8,128)S(1)} %get-tuple-element.52), channel_id=1, source_target_pairs={{16,0},{32,16},{48,32},{64,48},{80,64},{96,80},{112,96},{128,112},... | collective-permute-start | bytes 24584 | tf_op jit(solution)/shard_map/ppermute | solution.py:21
  347.2 4.5 collective-permute-start.13
  351.8 4.9 collective-permute-start.16
  356.7 2.4 collective-permute-start.17
  361.3 4.6 collective-permute-done.17
  366.0 1.9 collective-permute-start.19
  368.0 5.8 %collective-permute-start.20 = (f32[1,16,128]{2,1,0:T(8,128)S(1)}, f32[1,16,128]{2,1,0:T(8,128)S(1)}, u32[]{:S(2)}, u32[]{:S(2)}) collective-permute-start(f32[1,16,128]{2,1,0:T(8,128)S(1)} %get-tuple-element.29), channel_id=1, source_target_pairs={{16,0},{32,16},{48,32},{64,48},{80,64},{96,80},{112,96},{128,112},... | collective-permute-start | bytes 24584 | tf_op jit(solution)/shard_map/ppermute | solution.py:21
  375.7 5.8 %collective-permute-start.23 = (f32[1,16,128]{2,1,0:T(8,128)S(1)}, f32[1,16,128]{2,1,0:T(8,128)S(1)}, u32[]{:S(2)}, u32[]{:S(2)}) collective-permute-start(f32[1,16,128]{2,1,0:T(8,128)S(1)} %get-tuple-element.50), channel_id=1, source_target_pairs={{16,0},{32,16},{48,32},{64,48},{80,64},{96,80},{112,96},{128,112},... | collective-permute-start | bytes 24584 | tf_op jit(solution)/shard_map/ppermute | solution.py:21
  383.5 7.5 %collective-permute-start.24 = (f32[18,1,128]{2,1,0:T(1,128)S(1)}, f32[18,1,128]{2,1,0:T(1,128)S(1)}, u32[]{:S(2)}, u32[]{:S(2)}) collective-permute-start(f32[18,1,128]{2,1,0:T(1,128)S(1)} %get-tuple-element.38), channel_id=1, source_target_pairs={{1,0},{2,1},{3,2},{4,3},{5,4},{6,5},{7,6},{8,7},{9,8},{10,9},{11,1... | collective-permute-start | bytes 27656 | tf_op jit(solution)/shard_map/ppermute | solution.py:21
  395.1 5.1 %collective-permute-done.25 = f32[18,1,128]{2,1,0:T(1,128)S(1)} collective-permute-done((f32[18,1,128]{2,1,0:T(1,128)S(1)}, f32[18,1,128]{2,1,0:T(1,128)S(1)}, u32[]{:S(2)}, u32[]{:S(2)}) %collective-permute-start.25) | collective-permute-done | bytes 9248 | tf_op jit(solution)/shard_map/ppermute | solution.py:19
  400.4 1.9 collective-permute-start.27
  402.3 5.8 %collective-permute-start.28 = (f32[1,16,128]{2,1,0:T(8,128)S(1)}, f32[1,16,128]{2,1,0:T(8,128)S(1)}, u32[]{:S(2)}, u32[]{:S(2)}) collective-permute-start(f32[1,16,128]{2,1,0:T(8,128)S(1)} %get-tuple-element.27), channel_id=1, source_target_pairs={{16,0},{32,16},{48,32},{64,48},{80,64},{96,80},{112,96},{128,112},... | collective-permute-start | bytes 24584 | tf_op jit(solution)/shard_map/ppermute | solution.py:21
  410.1 5.8 %collective-permute-start.31 = (f32[1,16,128]{2,1,0:T(8,128)S(1)}, f32[1,16,128]{2,1,0:T(8,128)S(1)}, u32[]{:S(2)}, u32[]{:S(2)}) collective-permute-start(f32[1,16,128]{2,1,0:T(8,128)S(1)} %get-tuple-element.48), channel_id=1, source_target_pairs={{16,0},{32,16},{48,32},{64,48},{80,64},{96,80},{112,96},{128,112},... | collective-permute-start | bytes 24584 | tf_op jit(solution)/shard_map/ppermute | solution.py:21
  417.8 7.5 %collective-permute-start.32 = (f32[18,1,128]{2,1,0:T(1,128)S(1)}, f32[18,1,128]{2,1,0:T(1,128)S(1)}, u32[]{:S(2)}, u32[]{:S(2)}) collective-permute-start(f32[18,1,128]{2,1,0:T(1,128)S(1)} %get-tuple-element.36), channel_id=1, source_target_pairs={{1,0},{2,1},{3,2},{4,3},{5,4},{6,5},{7,6},{8,7},{9,8},{10,9},{11,1... | collective-permute-start | bytes 27656 | tf_op jit(solution)/shard_map/ppermute | solution.py:21
  429.4 5.1 %collective-permute-done.33 = f32[18,1,128]{2,1,0:T(1,128)S(1)} collective-permute-done((f32[18,1,128]{2,1,0:T(1,128)S(1)}, f32[18,1,128]{2,1,0:T(1,128)S(1)}, u32[]{:S(2)}, u32[]{:S(2)}) %collective-permute-start.33) | collective-permute-done | bytes 9248 | tf_op jit(solution)/shard_map/ppermute | solution.py:19
  434.7 1.9 collective-permute-start.35
  436.6 5.8 %collective-permute-start.36 = (f32[1,16,128]{2,1,0:T(8,128)S(1)}, f32[1,16,128]{2,1,0:T(8,128)S(1)}, u32[]{:S(2)}, u32[]{:S(2)}) collective-permute-start(f32[1,16,128]{2,1,0:T(8,128)S(1)} %get-tuple-element.25), channel_id=1, source_target_pairs={{16,0},{32,16},{48,32},{64,48},{80,64},{96,80},{112,96},{128,112},... | collective-permute-start | bytes 24584 | tf_op jit(solution)/shard_map/ppermute | solution.py:21
  444.4 5.8 %collective-permute-start.39 = (f32[1,16,128]{2,1,0:T(8,128)S(1)}, f32[1,16,128]{2,1,0:T(8,128)S(1)}, u32[]{:S(2)}, u32[]{:S(2)}) collective-permute-start(f32[1,16,128]{2,1,0:T(8,128)S(1)} %get-tuple-element.46), channel_id=1, source_target_pairs={{16,0},{32,16},{48,32},{64,48},{80,64},{96,80},{112,96},{128,112},... | collective-permute-start | bytes 24584 | tf_op jit(solution)/shard_map/ppermute | solution.py:21
  452.2 7.5 %collective-permute-start.40 = (f32[18,1,128]{2,1,0:T(1,128)S(1)}, f32[18,1,128]{2,1,0:T(1,128)S(1)}, u32[]{:S(2)}, u32[]{:S(2)}) collective-permute-start(f32[18,1,128]{2,1,0:T(1,128)S(1)} %get-tuple-element.34), channel_id=1, source_target_pairs={{1,0},{2,1},{3,2},{4,3},{5,4},{6,5},{7,6},{8,7},{9,8},{10,9},{11,1... | collective-permute-start | bytes 27656 | tf_op jit(solution)/shard_map/ppermute | solution.py:21
  463.7 5.1 %collective-permute-done.41 = f32[18,1,128]{2,1,0:T(1,128)S(1)} collective-permute-done((f32[18,1,128]{2,1,0:T(1,128)S(1)}, f32[18,1,128]{2,1,0:T(1,128)S(1)}, u32[]{:S(2)}, u32[]{:S(2)}) %collective-permute-start.41) | collective-permute-done | bytes 9248 | tf_op jit(solution)/shard_map/ppermute | solution.py:19
  469.0 1.9 collective-permute-start.43
  470.9 5.8 %collective-permute-start.44 = (f32[1,16,128]{2,1,0:T(8,128)S(1)}, f32[1,16,128]{2,1,0:T(8,128)S(1)}, u32[]{:S(2)}, u32[]{:S(2)}) collective-permute-start(f32[1,16,128]{2,1,0:T(8,128)S(1)} %get-tuple-element.23), channel_id=1, source_target_pairs={{16,0},{32,16},{48,32},{64,48},{80,64},{96,80},{112,96},{128,112},... | collective-permute-start | bytes 24584 | tf_op jit(solution)/shard_map/ppermute | solution.py:21
  478.7 5.8 %collective-permute-start.47 = (f32[1,16,128]{2,1,0:T(8,128)S(1)}, f32[1,16,128]{2,1,0:T(8,128)S(1)}, u32[]{:S(2)}, u32[]{:S(2)}) collective-permute-start(f32[1,16,128]{2,1,0:T(8,128)S(1)} %get-tuple-element.45), channel_id=1, source_target_pairs={{16,0},{32,16},{48,32},{64,48},{80,64},{96,80},{112,96},{128,112},... | collective-permute-start | bytes 24584 | tf_op jit(solution)/shard_map/ppermute | solution.py:21
  486.5 7.5 %collective-permute-start.48 = (f32[18,1,128]{2,1,0:T(1,128)S(1)}, f32[18,1,128]{2,1,0:T(1,128)S(1)}, u32[]{:S(2)}, u32[]{:S(2)}) collective-permute-start(f32[18,1,128]{2,1,0:T(1,128)S(1)} %get-tuple-element.32), channel_id=1, source_target_pairs={{1,0},{2,1},{3,2},{4,3},{5,4},{6,5},{7,6},{8,7},{9,8},{10,9},{11,1... | collective-permute-start | bytes 27656 | tf_op jit(solution)/shard_map/ppermute | solution.py:21
  496.1 7.1 %collective-permute-done.49 = f32[18,1,128]{2,1,0:T(1,128)S(1)} collective-permute-done((f32[18,1,128]{2,1,0:T(1,128)S(1)}, f32[18,1,128]{2,1,0:T(1,128)S(1)}, u32[]{:S(2)}, u32[]{:S(2)}) %collective-permute-start.49) | collective-permute-done | bytes 9248 | tf_op jit(solution)/shard_map/ppermute | solution.py:19
  (162 shorter events, 44.3 us)
Async XLA Ops:
  7.2 69.2 %all-gather.2.cloned.1.call-start = ((), (), s32[]{:S(2)}) async-start(), calls=%async_computation.1 | async-start | bytes 1081344 | tf_op jit(solution)/shard_map/all_gather | solution.py:62
  7.9 300.7 %reduce-scatter.2.cloned.1.call-start = ((), (), s32[]{:S(2)}) async-start(), calls=%async_computation.2 | async-start | bytes 2228224 | tf_op jit(solution)/shard_map/reduce_scatter | solution.py:85
  95.3 222.1 %collective-permute-start.4 = (f32[1,16,128]{2,1,0:T(8,128)S(1)}, f32[1,16,128]{2,1,0:T(8,128)S(1)}, u32[]{:S(2)}, u32[]{:S(2)}) collective-permute-start(f32[1,16,128]{2,1,0:T(8,128)S(1)} %broadcast.92), channel_id=1, source_target_pairs={{0,16},{16,32},{32,48},{48,64},{64,80},{80,96},{96,112},{112,128},... | collective-permute-start | bytes 24584 | tf_op jit(solution)/shard_map/ppermute | solution.py:19
  97.4 219.9 %collective-permute-start.5 = (f32[1,16,128]{2,1,0:T(8,128)S(1)}, f32[1,16,128]{2,1,0:T(8,128)S(1)}, u32[]{:S(2)}, u32[]{:S(2)}) collective-permute-start(f32[1,16,128]{2,1,0:T(8,128)S(1)} %broadcast.92), channel_id=1, source_target_pairs={{16,0},{32,16},{48,32},{64,48},{80,64},{96,80},{112,96},{128,112},... | collective-permute-start | bytes 24584 | tf_op jit(solution)/shard_map/ppermute | solution.py:21
  112.1 9.5 %collective-permute-start.2 = (f32[18,1]{1,0:T(8,128)S(1)}, f32[18,1]{1,0:T(8,128)S(1)}, u32[]{:S(2)}, u32[]{:S(2)}) collective-permute-start(f32[18,1]{1,0:T(8,128)S(1)} %get-tuple-element.56), channel_id=1, source_target_pairs={{0,1},{1,2},{2,3},{3,4},{4,5},{5,6},{6,7},{7,8},{8,9},{9,10},{10,1... | collective-permute-start | bytes 224 | tf_op jit(solution)/shard_map/ppermute | solution.py:19
  309.7 10.2 %collective-permute-start.7 = (f32[1,16,128]{2,1,0:T(8,128)S(1)}, f32[1,16,128]{2,1,0:T(8,128)S(1)}, u32[]{:S(2)}, u32[]{:S(2)}) collective-permute-start(f32[1,16,128]{2,1,0:T(8,128)S(1)} %get-tuple-element.55), channel_id=1, source_target_pairs={{0,16},{16,32},{32,48},{48,64},{64,80},{80,96},{96,112},{112,128},... | collective-permute-start | bytes 24584 | tf_op jit(solution)/shard_map/ppermute | solution.py:19
  311.6 8.3 %collective-permute-start.8 = (f32[1,16,128]{2,1,0:T(8,128)S(1)}, f32[1,16,128]{2,1,0:T(8,128)S(1)}, u32[]{:S(2)}, u32[]{:S(2)}) collective-permute-start(f32[1,16,128]{2,1,0:T(8,128)S(1)} %get-tuple-element.54), channel_id=1, source_target_pairs={{16,0},{32,16},{48,32},{64,48},{80,64},{96,80},{112,96},{128,112},... | collective-permute-start | bytes 24584 | tf_op jit(solution)/shard_map/ppermute | solution.py:21
  317.4 14.0 %collective-permute-start.6 = (f32[18,1,128]{2,1,0:T(1,128)S(1)}, f32[18,1,128]{2,1,0:T(1,128)S(1)}, u32[]{:S(2)}, u32[]{:S(2)}) collective-permute-start(f32[18,1,128]{2,1,0:T(1,128)S(1)} %pad_maximum_fusion.83), channel_id=1, source_target_pairs={{0,1},{1,2},{2,3},{3,4},{4,5},{5,6},{6,7},{7,8},{8,9},{9,10},{10,1... | collective-permute-start | bytes 27656 | tf_op jit(solution)/shard_map/ppermute | solution.py:19
  319.9 11.6 %collective-permute-start.10 = (f32[18,1,128]{2,1,0:T(1,128)S(1)}, f32[18,1,128]{2,1,0:T(1,128)S(1)}, u32[]{:S(2)}, u32[]{:S(2)}) collective-permute-start(f32[18,1,128]{2,1,0:T(1,128)S(1)} %get-tuple-element.43), channel_id=1, source_target_pairs={{0,1},{1,2},{2,3},{3,4},{4,5},{5,6},{6,7},{7,8},{8,9},{9,10},{10,1... | collective-permute-start | bytes 27656 | tf_op jit(solution)/shard_map/ppermute | solution.py:19
  329.5 29.6 %collective-permute-start.18 = (f32[1,16,128]{2,1,0:T(8,128)S(1)}, f32[1,16,128]{2,1,0:T(8,128)S(1)}, u32[]{:S(2)}, u32[]{:S(2)}) collective-permute-start(f32[1,16,128]{2,1,0:T(8,128)S(1)} %slice.550), channel_id=1, source_target_pairs={{0,16},{16,32},{32,48},{48,64},{64,80},{80,96},{96,112},{112,128},... | collective-permute-start | bytes 24584 | tf_op jit(solution)/shard_map/ppermute | solution.py:19
  331.6 15.5 %collective-permute-start.11 = (f32[1,16,128]{2,1,0:T(8,128)S(1)}, f32[1,16,128]{2,1,0:T(8,128)S(1)}, u32[]{:S(2)}, u32[]{:S(2)}) collective-permute-start(f32[1,16,128]{2,1,0:T(8,128)S(1)} %get-tuple-element.30), channel_id=1, source_target_pairs={{0,16},{16,32},{32,48},{48,64},{64,80},{80,96},{96,112},{112,128},... | collective-permute-start | bytes 24584 | tf_op jit(solution)/shard_map/ppermute | solution.py:19
  333.6 13.6 %collective-permute-start.12 = (f32[1,16,128]{2,1,0:T(8,128)S(1)}, f32[1,16,128]{2,1,0:T(8,128)S(1)}, u32[]{:S(2)}, u32[]{:S(2)}) collective-permute-start(f32[1,16,128]{2,1,0:T(8,128)S(1)} %get-tuple-element.31), channel_id=1, source_target_pairs={{16,0},{32,16},{48,32},{64,48},{80,64},{96,80},{112,96},{128,112},... | collective-permute-start | bytes 24584 | tf_op jit(solution)/shard_map/ppermute | solution.py:21
  339.5 12.3 %collective-permute-start.14 = (f32[1,16,128]{2,1,0:T(8,128)S(1)}, f32[1,16,128]{2,1,0:T(8,128)S(1)}, u32[]{:S(2)}, u32[]{:S(2)}) collective-permute-start(f32[1,16,128]{2,1,0:T(8,128)S(1)} %get-tuple-element.53), channel_id=1, source_target_pairs={{0,16},{16,32},{32,48},{48,64},{64,80},{80,96},{96,112},{112,128},... | collective-permute-start | bytes 24584 | tf_op jit(solution)/shard_map/ppermute | solution.py:19
  341.4 10.4 %collective-permute-start.15 = (f32[1,16,128]{2,1,0:T(8,128)S(1)}, f32[1,16,128]{2,1,0:T(8,128)S(1)}, u32[]{:S(2)}, u32[]{:S(2)}) collective-permute-start(f32[1,16,128]{2,1,0:T(8,128)S(1)} %get-tuple-element.52), channel_id=1, source_target_pairs={{16,0},{32,16},{48,32},{64,48},{80,64},{96,80},{112,96},{128,112},... | collective-permute-start | bytes 24584 | tf_op jit(solution)/shard_map/ppermute | solution.py:21
  347.2 14.0 %collective-permute-start.13 = (f32[18,1,128]{2,1,0:T(1,128)S(1)}, f32[18,1,128]{2,1,0:T(1,128)S(1)}, u32[]{:S(2)}, u32[]{:S(2)}) collective-permute-start(f32[18,1,128]{2,1,0:T(1,128)S(1)} %pad_maximum_fusion.78), channel_id=1, source_target_pairs={{0,1},{1,2},{2,3},{3,4},{4,5},{5,6},{6,7},{7,8},{8,9},{9,10},{10,1... | collective-permute-start | bytes 27656 | tf_op jit(solution)/shard_map/ppermute | solution.py:19
  351.8 9.5 %collective-permute-start.16 = (f32[18,1,128]{2,1,0:T(1,128)S(1)}, f32[18,1,128]{2,1,0:T(1,128)S(1)}, u32[]{:S(2)}, u32[]{:S(2)}) collective-permute-start(f32[18,1,128]{2,1,0:T(1,128)S(1)} %get-tuple-element.40), channel_id=1, source_target_pairs={{1,0},{2,1},{3,2},{4,3},{5,4},{6,5},{7,6},{8,7},{9,8},{10,9},{11,1... | collective-permute-start | bytes 27656 | tf_op jit(solution)/shard_map/ppermute | solution.py:21
  356.7 9.2 %collective-permute-start.17 = (f32[18,1,128]{2,1,0:T(1,128)S(1)}, f32[18,1,128]{2,1,0:T(1,128)S(1)}, u32[]{:S(2)}, u32[]{:S(2)}) collective-permute-start(f32[18,1,128]{2,1,0:T(1,128)S(1)} %get-tuple-element.41), channel_id=1, source_target_pairs={{0,1},{1,2},{2,3},{3,4},{4,5},{5,6},{6,7},{7,8},{8,9},{9,10},{10,1... | collective-permute-start | bytes 27656 | tf_op jit(solution)/shard_map/ppermute | solution.py:19
  359.3 33.7 %collective-permute-start.26 = (f32[1,16,128]{2,1,0:T(8,128)S(1)}, f32[1,16,128]{2,1,0:T(8,128)S(1)}, u32[]{:S(2)}, u32[]{:S(2)}) collective-permute-start(f32[1,16,128]{2,1,0:T(8,128)S(1)} %slice.561), channel_id=1, source_target_pairs={{0,16},{16,32},{32,48},{48,64},{64,80},{80,96},{96,112},{112,128},... | collective-permute-start | bytes 24584 | tf_op jit(solution)/shard_map/ppermute | solution.py:19
  366.0 15.5 %collective-permute-start.19 = (f32[1,16,128]{2,1,0:T(8,128)S(1)}, f32[1,16,128]{2,1,0:T(8,128)S(1)}, u32[]{:S(2)}, u32[]{:S(2)}) collective-permute-start(f32[1,16,128]{2,1,0:T(8,128)S(1)} %get-tuple-element.28), channel_id=1, source_target_pairs={{0,16},{16,32},{32,48},{48,64},{64,80},{80,96},{96,112},{112,128},... | collective-permute-start | bytes 24584 | tf_op jit(solution)/shard_map/ppermute | solution.py:19
  368.0 13.5 %collective-permute-start.20 = (f32[1,16,128]{2,1,0:T(8,128)S(1)}, f32[1,16,128]{2,1,0:T(8,128)S(1)}, u32[]{:S(2)}, u32[]{:S(2)}) collective-permute-start(f32[1,16,128]{2,1,0:T(8,128)S(1)} %get-tuple-element.29), channel_id=1, source_target_pairs={{16,0},{32,16},{48,32},{64,48},{80,64},{96,80},{112,96},{128,112},... | collective-permute-start | bytes 24584 | tf_op jit(solution)/shard_map/ppermute | solution.py:21
  373.8 9.7 %collective-permute-start.22 = (f32[1,16,128]{2,1,0:T(8,128)S(1)}, f32[1,16,128]{2,1,0:T(8,128)S(1)}, u32[]{:S(2)}, u32[]{:S(2)}) collective-permute-start(f32[1,16,128]{2,1,0:T(8,128)S(1)} %get-tuple-element.51), channel_id=1, source_target_pairs={{0,16},{16,32},{32,48},{48,64},{64,80},{80,96},{96,112},{112,128},... | collective-permute-start | bytes 24584 | tf_op jit(solution)/shard_map/ppermute | solution.py:19
  375.7 7.7 %collective-permute-start.23 = (f32[1,16,128]{2,1,0:T(8,128)S(1)}, f32[1,16,128]{2,1,0:T(8,128)S(1)}, u32[]{:S(2)}, u32[]{:S(2)}) collective-permute-start(f32[1,16,128]{2,1,0:T(8,128)S(1)} %get-tuple-element.50), channel_id=1, source_target_pairs={{16,0},{32,16},{48,32},{64,48},{80,64},{96,80},{112,96},{128,112},... | collective-permute-start | bytes 24584 | tf_op jit(solution)/shard_map/ppermute | solution.py:21
  381.5 13.5 %collective-permute-start.21 = (f32[18,1,128]{2,1,0:T(1,128)S(1)}, f32[18,1,128]{2,1,0:T(1,128)S(1)}, u32[]{:S(2)}, u32[]{:S(2)}) collective-permute-start(f32[18,1,128]{2,1,0:T(1,128)S(1)} %pad_maximum_fusion.73), channel_id=1, source_target_pairs={{0,1},{1,2},{2,3},{3,4},{4,5},{5,6},{6,7},{7,8},{8,9},{9,10},{10,1... | collective-permute-start | bytes 27656 | tf_op jit(solution)/shard_map/ppermute | solution.py:19
  383.5 11.6 %collective-permute-start.24 = (f32[18,1,128]{2,1,0:T(1,128)S(1)}, f32[18,1,128]{2,1,0:T(1,128)S(1)}, u32[]{:S(2)}, u32[]{:S(2)}) collective-permute-start(f32[18,1,128]{2,1,0:T(1,128)S(1)} %get-tuple-element.38), channel_id=1, source_target_pairs={{1,0},{2,1},{3,2},{4,3},{5,4},{6,5},{7,6},{8,7},{9,8},{10,9},{11,1... | collective-permute-start | bytes 27656 | tf_op jit(solution)/shard_map/ppermute | solution.py:21
  391.1 9.2 %collective-permute-start.25 = (f32[18,1,128]{2,1,0:T(1,128)S(1)}, f32[18,1,128]{2,1,0:T(1,128)S(1)}, u32[]{:S(2)}, u32[]{:S(2)}) collective-permute-start(f32[18,1,128]{2,1,0:T(1,128)S(1)} %get-tuple-element.39), channel_id=1, source_target_pairs={{0,1},{1,2},{2,3},{3,4},{4,5},{5,6},{6,7},{7,8},{8,9},{9,10},{10,1... | collective-permute-start | bytes 27656 | tf_op jit(solution)/shard_map/ppermute | solution.py:19
  393.1 34.2 %collective-permute-start.34 = (f32[1,16,128]{2,1,0:T(8,128)S(1)}, f32[1,16,128]{2,1,0:T(8,128)S(1)}, u32[]{:S(2)}, u32[]{:S(2)}) collective-permute-start(f32[1,16,128]{2,1,0:T(8,128)S(1)} %slice.572), channel_id=1, source_target_pairs={{0,16},{16,32},{32,48},{48,64},{64,80},{80,96},{96,112},{112,128},... | collective-permute-start | bytes 24584 | tf_op jit(solution)/shard_map/ppermute | solution.py:19
  400.4 15.5 %collective-permute-start.27 = (f32[1,16,128]{2,1,0:T(8,128)S(1)}, f32[1,16,128]{2,1,0:T(8,128)S(1)}, u32[]{:S(2)}, u32[]{:S(2)}) collective-permute-start(f32[1,16,128]{2,1,0:T(8,128)S(1)} %get-tuple-element.26), channel_id=1, source_target_pairs={{0,16},{16,32},{32,48},{48,64},{64,80},{80,96},{96,112},{112,128},... | collective-permute-start | bytes 24584 | tf_op jit(solution)/shard_map/ppermute | solution.py:19
  402.3 13.5 %collective-permute-start.28 = (f32[1,16,128]{2,1,0:T(8,128)S(1)}, f32[1,16,128]{2,1,0:T(8,128)S(1)}, u32[]{:S(2)}, u32[]{:S(2)}) collective-permute-start(f32[1,16,128]{2,1,0:T(8,128)S(1)} %get-tuple-element.27), channel_id=1, source_target_pairs={{16,0},{32,16},{48,32},{64,48},{80,64},{96,80},{112,96},{128,112},... | collective-permute-start | bytes 24584 | tf_op jit(solution)/shard_map/ppermute | solution.py:21
  408.1 9.7 %collective-permute-start.30 = (f32[1,16,128]{2,1,0:T(8,128)S(1)}, f32[1,16,128]{2,1,0:T(8,128)S(1)}, u32[]{:S(2)}, u32[]{:S(2)}) collective-permute-start(f32[1,16,128]{2,1,0:T(8,128)S(1)} %get-tuple-element.49), channel_id=1, source_target_pairs={{0,16},{16,32},{32,48},{48,64},{64,80},{80,96},{96,112},{112,128},... | collective-permute-start | bytes 24584 | tf_op jit(solution)/shard_map/ppermute | solution.py:19
  410.1 7.7 %collective-permute-start.31 = (f32[1,16,128]{2,1,0:T(8,128)S(1)}, f32[1,16,128]{2,1,0:T(8,128)S(1)}, u32[]{:S(2)}, u32[]{:S(2)}) collective-permute-start(f32[1,16,128]{2,1,0:T(8,128)S(1)} %get-tuple-element.48), channel_id=1, source_target_pairs={{16,0},{32,16},{48,32},{64,48},{80,64},{96,80},{112,96},{128,112},... | collective-permute-start | bytes 24584 | tf_op jit(solution)/shard_map/ppermute | solution.py:21
  415.9 13.5 %collective-permute-start.29 = (f32[18,1,128]{2,1,0:T(1,128)S(1)}, f32[18,1,128]{2,1,0:T(1,128)S(1)}, u32[]{:S(2)}, u32[]{:S(2)}) collective-permute-start(f32[18,1,128]{2,1,0:T(1,128)S(1)} %pad_maximum_fusion.68), channel_id=1, source_target_pairs={{0,1},{1,2},{2,3},{3,4},{4,5},{5,6},{6,7},{7,8},{8,9},{9,10},{10,1... | collective-permute-start | bytes 27656 | tf_op jit(solution)/shard_map/ppermute | solution.py:19
  417.8 11.6 %collective-permute-start.32 = (f32[18,1,128]{2,1,0:T(1,128)S(1)}, f32[18,1,128]{2,1,0:T(1,128)S(1)}, u32[]{:S(2)}, u32[]{:S(2)}) collective-permute-start(f32[18,1,128]{2,1,0:T(1,128)S(1)} %get-tuple-element.36), channel_id=1, source_target_pairs={{1,0},{2,1},{3,2},{4,3},{5,4},{6,5},{7,6},{8,7},{9,8},{10,9},{11,1... | collective-permute-start | bytes 27656 | tf_op jit(solution)/shard_map/ppermute | solution.py:21
  425.4 9.2 %collective-permute-start.33 = (f32[18,1,128]{2,1,0:T(1,128)S(1)}, f32[18,1,128]{2,1,0:T(1,128)S(1)}, u32[]{:S(2)}, u32[]{:S(2)}) collective-permute-start(f32[18,1,128]{2,1,0:T(1,128)S(1)} %get-tuple-element.37), channel_id=1, source_target_pairs={{0,1},{1,2},{2,3},{3,4},{4,5},{5,6},{6,7},{7,8},{8,9},{9,10},{10,1... | collective-permute-start | bytes 27656 | tf_op jit(solution)/shard_map/ppermute | solution.py:19
  427.5 34.2 %collective-permute-start.42 = (f32[1,16,128]{2,1,0:T(8,128)S(1)}, f32[1,16,128]{2,1,0:T(8,128)S(1)}, u32[]{:S(2)}, u32[]{:S(2)}) collective-permute-start(f32[1,16,128]{2,1,0:T(8,128)S(1)} %slice.583), channel_id=1, source_target_pairs={{0,16},{16,32},{32,48},{48,64},{64,80},{80,96},{96,112},{112,128},... | collective-permute-start | bytes 24584 | tf_op jit(solution)/shard_map/ppermute | solution.py:19
  434.7 15.5 %collective-permute-start.35 = (f32[1,16,128]{2,1,0:T(8,128)S(1)}, f32[1,16,128]{2,1,0:T(8,128)S(1)}, u32[]{:S(2)}, u32[]{:S(2)}) collective-permute-start(f32[1,16,128]{2,1,0:T(8,128)S(1)} %get-tuple-element.24), channel_id=1, source_target_pairs={{0,16},{16,32},{32,48},{48,64},{64,80},{80,96},{96,112},{112,128},... | collective-permute-start | bytes 24584 | tf_op jit(solution)/shard_map/ppermute | solution.py:19
  436.6 13.5 %collective-permute-start.36 = (f32[1,16,128]{2,1,0:T(8,128)S(1)}, f32[1,16,128]{2,1,0:T(8,128)S(1)}, u32[]{:S(2)}, u32[]{:S(2)}) collective-permute-start(f32[1,16,128]{2,1,0:T(8,128)S(1)} %get-tuple-element.25), channel_id=1, source_target_pairs={{16,0},{32,16},{48,32},{64,48},{80,64},{96,80},{112,96},{128,112},... | collective-permute-start | bytes 24584 | tf_op jit(solution)/shard_map/ppermute | solution.py:21
  442.5 9.7 %collective-permute-start.38 = (f32[1,16,128]{2,1,0:T(8,128)S(1)}, f32[1,16,128]{2,1,0:T(8,128)S(1)}, u32[]{:S(2)}, u32[]{:S(2)}) collective-permute-start(f32[1,16,128]{2,1,0:T(8,128)S(1)} %get-tuple-element.47), channel_id=1, source_target_pairs={{0,16},{16,32},{32,48},{48,64},{64,80},{80,96},{96,112},{112,128},... | collective-permute-start | bytes 24584 | tf_op jit(solution)/shard_map/ppermute | solution.py:19
  444.4 7.7 %collective-permute-start.39 = (f32[1,16,128]{2,1,0:T(8,128)S(1)}, f32[1,16,128]{2,1,0:T(8,128)S(1)}, u32[]{:S(2)}, u32[]{:S(2)}) collective-permute-start(f32[1,16,128]{2,1,0:T(8,128)S(1)} %get-tuple-element.46), channel_id=1, source_target_pairs={{16,0},{32,16},{48,32},{64,48},{80,64},{96,80},{112,96},{128,112},... | collective-permute-start | bytes 24584 | tf_op jit(solution)/shard_map/ppermute | solution.py:21
  450.2 13.5 %collective-permute-start.37 = (f32[18,1,128]{2,1,0:T(1,128)S(1)}, f32[18,1,128]{2,1,0:T(1,128)S(1)}, u32[]{:S(2)}, u32[]{:S(2)}) collective-permute-start(f32[18,1,128]{2,1,0:T(1,128)S(1)} %pad_maximum_fusion.63), channel_id=1, source_target_pairs={{0,1},{1,2},{2,3},{3,4},{4,5},{5,6},{6,7},{7,8},{8,9},{9,10},{10,1... | collective-permute-start | bytes 27656 | tf_op jit(solution)/shard_map/ppermute | solution.py:19
  452.2 11.6 %collective-permute-start.40 = (f32[18,1,128]{2,1,0:T(1,128)S(1)}, f32[18,1,128]{2,1,0:T(1,128)S(1)}, u32[]{:S(2)}, u32[]{:S(2)}) collective-permute-start(f32[18,1,128]{2,1,0:T(1,128)S(1)} %get-tuple-element.34), channel_id=1, source_target_pairs={{1,0},{2,1},{3,2},{4,3},{5,4},{6,5},{7,6},{8,7},{9,8},{10,9},{11,1... | collective-permute-start | bytes 27656 | tf_op jit(solution)/shard_map/ppermute | solution.py:21
  459.7 9.2 %collective-permute-start.41 = (f32[18,1,128]{2,1,0:T(1,128)S(1)}, f32[18,1,128]{2,1,0:T(1,128)S(1)}, u32[]{:S(2)}, u32[]{:S(2)}) collective-permute-start(f32[18,1,128]{2,1,0:T(1,128)S(1)} %get-tuple-element.35), channel_id=1, source_target_pairs={{0,1},{1,2},{2,3},{3,4},{4,5},{5,6},{6,7},{7,8},{8,9},{9,10},{10,1... | collective-permute-start | bytes 27656 | tf_op jit(solution)/shard_map/ppermute | solution.py:19
  461.8 34.2 %collective-permute-start.50 = (f32[1,16,128]{2,1,0:T(8,128)S(1)}, f32[1,16,128]{2,1,0:T(8,128)S(1)}, u32[]{:S(2)}, u32[]{:S(2)}) collective-permute-start(f32[1,16,128]{2,1,0:T(8,128)S(1)} %slice.594), channel_id=1, source_target_pairs={{0,16},{16,32},{32,48},{48,64},{64,80},{80,96},{96,112},{112,128},... | collective-permute-start | bytes 24584 | tf_op jit(solution)/shard_map/ppermute | solution.py:19
  469.0 15.5 %collective-permute-start.43 = (f32[1,16,128]{2,1,0:T(8,128)S(1)}, f32[1,16,128]{2,1,0:T(8,128)S(1)}, u32[]{:S(2)}, u32[]{:S(2)}) collective-permute-start(f32[1,16,128]{2,1,0:T(8,128)S(1)} %get-tuple-element.22), channel_id=1, source_target_pairs={{0,16},{16,32},{32,48},{48,64},{64,80},{80,96},{96,112},{112,128},... | collective-permute-start | bytes 24584 | tf_op jit(solution)/shard_map/ppermute | solution.py:19
  470.9 13.5 %collective-permute-start.44 = (f32[1,16,128]{2,1,0:T(8,128)S(1)}, f32[1,16,128]{2,1,0:T(8,128)S(1)}, u32[]{:S(2)}, u32[]{:S(2)}) collective-permute-start(f32[1,16,128]{2,1,0:T(8,128)S(1)} %get-tuple-element.23), channel_id=1, source_target_pairs={{16,0},{32,16},{48,32},{64,48},{80,64},{96,80},{112,96},{128,112},... | collective-permute-start | bytes 24584 | tf_op jit(solution)/shard_map/ppermute | solution.py:21
  476.8 9.7 %collective-permute-start.46 = (f32[1,16,128]{2,1,0:T(8,128)S(1)}, f32[1,16,128]{2,1,0:T(8,128)S(1)}, u32[]{:S(2)}, u32[]{:S(2)}) collective-permute-start(f32[1,16,128]{2,1,0:T(8,128)S(1)} %get-tuple-element.44), channel_id=1, source_target_pairs={{0,16},{16,32},{32,48},{48,64},{64,80},{80,96},{96,112},{112,128},... | collective-permute-start | bytes 24584 | tf_op jit(solution)/shard_map/ppermute | solution.py:19
  484.5 11.6 %collective-permute-start.45 = (f32[18,1,128]{2,1,0:T(1,128)S(1)}, f32[18,1,128]{2,1,0:T(1,128)S(1)}, u32[]{:S(2)}, u32[]{:S(2)}) collective-permute-start(f32[18,1,128]{2,1,0:T(1,128)S(1)} %pad_maximum_fusion.58), channel_id=1, source_target_pairs={{0,1},{1,2},{2,3},{3,4},{4,5},{5,6},{6,7},{7,8},{8,9},{9,10},{10,1... | collective-permute-start | bytes 27656 | tf_op jit(solution)/shard_map/ppermute | solution.py:19
  486.5 9.6 %collective-permute-start.48 = (f32[18,1,128]{2,1,0:T(1,128)S(1)}, f32[18,1,128]{2,1,0:T(1,128)S(1)}, u32[]{:S(2)}, u32[]{:S(2)}) collective-permute-start(f32[18,1,128]{2,1,0:T(1,128)S(1)} %get-tuple-element.32), channel_id=1, source_target_pairs={{1,0},{2,1},{3,2},{4,3},{5,4},{6,5},{7,6},{8,7},{9,8},{10,9},{11,1... | collective-permute-start | bytes 27656 | tf_op jit(solution)/shard_map/ppermute | solution.py:21
  494.0 9.2 %collective-permute-start.49 = (f32[18,1,128]{2,1,0:T(1,128)S(1)}, f32[18,1,128]{2,1,0:T(1,128)S(1)}, u32[]{:S(2)}, u32[]{:S(2)}) collective-permute-start(f32[18,1,128]{2,1,0:T(1,128)S(1)} %get-tuple-element.33), channel_id=1, source_target_pairs={{0,1},{1,2},{2,3},{3,4},{4,5},{5,6},{6,7},{7,8},{8,9},{9,10},{10,1... | collective-permute-start | bytes 27656 | tf_op jit(solution)/shard_map/ppermute | solution.py:19
  (16 other events, 248.5 us)
Sparse Core Ops, SparseCore 0:
  10.2 66.1 all-gather.1
  95.4 213.1 reduce-scatter.1
where the time goes:
time: 513 us; the launch traced here: 511 us
  waiting for transfers between devices  283 us (55%)
  starting transfers between devices  188 us (37%)
  between operations  15.3 us (3%)
  local copies, waits for them, and re-layouts  9.79 us (2%)
  matrix products  9.23 us (2%)
  other arithmetic  5.81 us (1%)
    reduce_scatter x1, waiting for transfers between devices, on_device(): summed = lax.psum_scatter(ordered, 'fault', scatter_dimension=0, tiled=True)  184 us
    ppermute x20, starting transfers between devices, extended(): lax.ppermute(head, axis, [((i + 1) % count, i) for i in range(ends)])  120 us
    ppermute x31, starting transfers between devices, extended(): lax.ppermute(tail, axis, [(i, (i + 1) % count) for i in range(ends)])  68.3 us
    all_gather x1, waiting for transfers between devices, on_device(): gathered = lax.all_gather(slip_rate, 'sea', axis=0, tiled=True)  66.4 us
    ppermute x31, waiting for transfers between devices, extended(): lax.ppermute(tail, axis, [(i, (i + 1) % count) for i in range(ends)])  27.2 us
  transfers between devices with their start and end apart: 53, of which 9 were waited for; matrix products, arithmetic and copies ran while one was open for 1% of the time, Pallas kernels for 0%

commit v1 on v0

--- a/solution.py
+++ b/solution.py
@@ -59,7 +59,9 @@
     members = slip_rate.shape[1]
     leaf_count = brick_y * brick_x * fault_count // leaf_size
     targets = jnp.arange(leaf_count)
-    gathered = lax.all_gather(slip_rate, "sea", axis=0, tiled=True)
+    gathered = jnp.concatenate(
+        lax.all_to_all(jnp.stack([slip_rate] * lax.axis_size("sea")), "sea", 0, 0), axis=0
+    )
     leaves = gathered.reshape(-1, leaf_size, members)
     near_slip = leaves[near_cols[0, 0]]
     near_term = jnp.einsum(

time: 513 us -> 476 us (0.928)
  waiting for transfers between devices: 283 us -> 239 us
  starting transfers between devices: 188 us -> 196 us
    all_gather x1 -> x0, waiting for transfers between devices: 66.4 us -> none  [on_device(): gathered = lax.all_gather(slip_rate, 'sea', axis=0, tiled=True)]
    all_to_all x0 -> x1, waiting for transfers between devices: none -> 24 us  [on_device(): lax.all_to_all(jnp.stack([slip_rate] * lax.axis_size('sea')), 'sea', 0, 0)]
    all_to_all x0 -> x1, starting transfers between devices: none -> 8.3 us  [on_device(): lax.all_to_all(jnp.stack([slip_rate] * lax.axis_size('sea')), 'sea', 0, 0)]
where the time goes in v1:
time: 476 us; the launch traced here: 474 us
  waiting for transfers between devices  239 us (50%)
  starting transfers between devices  196 us (41%)
  between operations  15.4 us (3%)
  local copies, waits for them, and re-layouts  10.9 us (2%)
  matrix products  8.48 us (2%)
    reduce_scatter x1, waiting for transfers between devices, on_device(): summed = lax.psum_scatter(ordered, 'fault', scatter_dimension=0, tiled=True)  185 us
    ppermute x20, starting transfers between devices, extended(): lax.ppermute(head, axis, [((i + 1) % count, i) for i in range(ends)])  120 us
    ppermute x31, starting transfers between devices, extended(): lax.ppermute(tail, axis, [(i, (i + 1) % count) for i in range(ends)])  68.4 us
    ppermute x31, waiting for transfers between devices, extended(): lax.ppermute(tail, axis, [(i, (i + 1) % count) for i in range(ends)])  27.2 us
    all_to_all x1, waiting for transfers between devices, on_device(): lax.all_to_all(jnp.stack([slip_rate] * lax.axis_size('sea')), 'sea', 0, 0)  24 us
  transfers between devices with their start and end apart: 53, of which 9 were waited for; matrix products, arithmetic and copies ran while one was open for 1% of the time, Pallas kernels for 0%

profile of v1, /device:TPU:288, one launch (start us, length us, event | category | flops | bytes accessed | tf_op | source)
XLA Modules:
  0.0 474.5 jit_solution(16885931649520270922)
XLA Ops:
  7.2 2.1 stack.2
  9.3 8.3 %all-to-all-start = ((bf16[32,128,128]{2,1,0:T(8,128)(2,1)}), bf16[32,128,128]{2,1,0:T(8,128)(2,1)S(1)}, u32[]{:S(2)}, u32[]{:S(2)}) async-start(bf16[32,128,128]{2,1,0:T(8,128)(2,1)} %stack.2), calls=%async_computation | async-start | bytes 2097152 | tf_op jit(solution)/shard_map/all_to_all | solution.py:63
  17.8 24.0 %all-to-all-done = bf16[32,128,128]{2,1,0:T(8,128)(2,1)S(1)} async-done(((bf16[32,128,128]{2,1,0:T(8,128)(2,1)}), bf16[32,128,128]{2,1,0:T(8,128)(2,1)S(1)}, u32[]{:S(2)}, u32[]{:S(2)}) %all-to-all-start) | async-done | bytes 1048608 | tf_op jit(solution)/shard_map/all_to_all | solution.py:63
  41.8 2.0 gather_fusion.1
  43.8 4.1 fusion.5
  47.9 3.5 copy.17
  55.0 2.0 fusion.2
  57.0 2.0 copy.19
  59.0 2.5 collective-permute-start.4
  61.5 5.2 %collective-permute-start.5 = (f32[1,16,128]{2,1,0:T(8,128)S(1)}, f32[1,16,128]{2,1,0:T(8,128)S(1)}, u32[]{:S(2)}, u32[]{:S(2)}) collective-permute-start(f32[1,16,128]{2,1,0:T(8,128)S(1)} %broadcast.94), channel_id=1, source_target_pairs={{16,0},{32,16},{48,32},{64,48},{80,64},{96,80},{112,96},{128,112},... | collective-permute-start | bytes 24584 | tf_op jit(solution)/shard_map/ppermute | solution.py:21
  68.7 5.8 %collective-permute-start.1 = (f32[1,16]{1,0:T(1,128)S(1)}, f32[1,16]{1,0:T(1,128)S(1)}, u32[]{:S(2)}, u32[]{:S(2)}) collective-permute-start(f32[1,16]{1,0:T(1,128)S(1)} %get-tuple-element.58), channel_id=1, source_target_pairs={{16,0},{32,16},{48,32},{64,48},{80,64},{96,80},{112,96},{128,112},... | collective-permute-start | bytes 200 | tf_op jit(solution)/shard_map/ppermute | solution.py:21
  75.8 4.6 collective-permute-start.2
  80.4 4.8 %collective-permute-start.3 = (f32[18,1]{1,0:T(8,128)S(1)}, f32[18,1]{1,0:T(8,128)S(1)}, u32[]{:S(2)}, u32[]{:S(2)}) collective-permute-start(f32[18,1]{1,0:T(8,128)S(1)} %get-tuple-element.57), channel_id=1, source_target_pairs={{1,0},{2,1},{3,2},{4,3},{5,4},{6,5},{7,6},{8,7},{9,8},{10,9},{11,1... | collective-permute-start | bytes 224 | tf_op jit(solution)/shard_map/ppermute | solution.py:21
  85.3 2.2 collective-permute-done.3
  87.6 184.6 %reduce-scatter.2.cloned.1.call-done = f32[1,16,16,128]{3,2,1,0:T(8,128)} async-done(((f32[16,16,16,128]{3,2,1,0:T(8,128)}), f32[1,16,16,128]{3,2,1,0:T(8,128)}) %reduce-scatter.2.cloned.1.call-update) | async-done | bytes 131088 | tf_op jit(solution)/shard_map/reduce_scatter | solution.py:87
  273.3 1.9 collective-permute-start.7
  275.2 5.8 %collective-permute-start.8 = (f32[1,16,128]{2,1,0:T(8,128)S(1)}, f32[1,16,128]{2,1,0:T(8,128)S(1)}, u32[]{:S(2)}, u32[]{:S(2)}) collective-permute-start(f32[1,16,128]{2,1,0:T(8,128)S(1)} %get-tuple-element.54), channel_id=1, source_target_pairs={{16,0},{32,16},{48,32},{64,48},{80,64},{96,80},{112,96},{128,112},... | collective-permute-start | bytes 24584 | tf_op jit(solution)/shard_map/ppermute | solution.py:21
  281.1 2.5 collective-permute-start.6
  283.6 3.8 collective-permute-start.10
  287.4 5.6 %collective-permute-start.9 = (f32[18,1,128]{2,1,0:T(1,128)S(1)}, f32[18,1,128]{2,1,0:T(1,128)S(1)}, u32[]{:S(2)}, u32[]{:S(2)}) collective-permute-start(f32[18,1,128]{2,1,0:T(1,128)S(1)} %get-tuple-element.42), channel_id=1, source_target_pairs={{1,0},{2,1},{3,2},{4,3},{5,4},{6,5},{7,6},{8,7},{9,8},{10,9},{11,1... | collective-permute-start | bytes 27656 | tf_op jit(solution)/shard_map/ppermute | solution.py:21
  297.2 5.8 %collective-permute-start.12 = (f32[1,16,128]{2,1,0:T(8,128)S(1)}, f32[1,16,128]{2,1,0:T(8,128)S(1)}, u32[]{:S(2)}, u32[]{:S(2)}) collective-permute-start(f32[1,16,128]{2,1,0:T(8,128)S(1)} %get-tuple-element.31), channel_id=1, source_target_pairs={{16,0},{32,16},{48,32},{64,48},{80,64},{96,80},{112,96},{128,112},... | collective-permute-start | bytes 24584 | tf_op jit(solution)/shard_map/ppermute | solution.py:21
  305.1 5.8 %collective-permute-start.15 = (f32[1,16,128]{2,1,0:T(8,128)S(1)}, f32[1,16,128]{2,1,0:T(8,128)S(1)}, u32[]{:S(2)}, u32[]{:S(2)}) collective-permute-start(f32[1,16,128]{2,1,0:T(8,128)S(1)} %get-tuple-element.52), channel_id=1, source_target_pairs={{16,0},{32,16},{48,32},{64,48},{80,64},{96,80},{112,96},{128,112},... | collective-permute-start | bytes 24584 | tf_op jit(solution)/shard_map/ppermute | solution.py:21
  310.9 4.5 collective-permute-start.13
  315.4 5.0 %collective-permute-start.16 = (f32[18,1,128]{2,1,0:T(1,128)S(1)}, f32[18,1,128]{2,1,0:T(1,128)S(1)}, u32[]{:S(2)}, u32[]{:S(2)}) collective-permute-start(f32[18,1,128]{2,1,0:T(1,128)S(1)} %get-tuple-element.40), channel_id=1, source_target_pairs={{1,0},{2,1},{3,2},{4,3},{5,4},{6,5},{7,6},{8,7},{9,8},{10,9},{11,1... | collective-permute-start | bytes 27656 | tf_op jit(solution)/shard_map/ppermute | solution.py:21
  320.4 2.4 collective-permute-start.17
  324.9 4.7 collective-permute-done.17
  329.7 1.9 collective-permute-start.19
  331.6 5.8 %collective-permute-start.20 = (f32[1,16,128]{2,1,0:T(8,128)S(1)}, f32[1,16,128]{2,1,0:T(8,128)S(1)}, u32[]{:S(2)}, u32[]{:S(2)}) collective-permute-start(f32[1,16,128]{2,1,0:T(8,128)S(1)} %get-tuple-element.29), channel_id=1, source_target_pairs={{16,0},{32,16},{48,32},{64,48},{80,64},{96,80},{112,96},{128,112},... | collective-permute-start | bytes 24584 | tf_op jit(solution)/shard_map/ppermute | solution.py:21
  339.4 5.8 %collective-permute-start.23 = (f32[1,16,128]{2,1,0:T(8,128)S(1)}, f32[1,16,128]{2,1,0:T(8,128)S(1)}, u32[]{:S(2)}, u32[]{:S(2)}) collective-permute-start(f32[1,16,128]{2,1,0:T(8,128)S(1)} %get-tuple-element.50), channel_id=1, source_target_pairs={{16,0},{32,16},{48,32},{64,48},{80,64},{96,80},{112,96},{128,112},... | collective-permute-start | bytes 24584 | tf_op jit(solution)/shard_map/ppermute | solution.py:21
  345.2 1.9 collective-permute-start.21
  347.1 7.5 %collective-permute-start.24 = (f32[18,1,128]{2,1,0:T(1,128)S(1)}, f32[18,1,128]{2,1,0:T(1,128)S(1)}, u32[]{:S(2)}, u32[]{:S(2)}) collective-permute-start(f32[18,1,128]{2,1,0:T(1,128)S(1)} %get-tuple-element.38), channel_id=1, source_target_pairs={{1,0},{2,1},{3,2},{4,3},{5,4},{6,5},{7,6},{8,7},{9,8},{10,9},{11,1... | collective-permute-start | bytes 27656 | tf_op jit(solution)/shard_map/ppermute | solution.py:21
  358.7 5.1 %collective-permute-done.25 = f32[18,1,128]{2,1,0:T(1,128)S(1)} collective-permute-done((f32[18,1,128]{2,1,0:T(1,128)S(1)}, f32[18,1,128]{2,1,0:T(1,128)S(1)}, u32[]{:S(2)}, u32[]{:S(2)}) %collective-permute-start.25) | collective-permute-done | bytes 9248 | tf_op jit(solution)/shard_map/ppermute | solution.py:19
  364.0 1.9 collective-permute-start.27
  365.9 5.8 %collective-permute-start.28 = (f32[1,16,128]{2,1,0:T(8,128)S(1)}, f32[1,16,128]{2,1,0:T(8,128)S(1)}, u32[]{:S(2)}, u32[]{:S(2)}) collective-permute-start(f32[1,16,128]{2,1,0:T(8,128)S(1)} %get-tuple-element.27), channel_id=1, source_target_pairs={{16,0},{32,16},{48,32},{64,48},{80,64},{96,80},{112,96},{128,112},... | collective-permute-start | bytes 24584 | tf_op jit(solution)/shard_map/ppermute | solution.py:21
  373.7 5.8 %collective-permute-start.31 = (f32[1,16,128]{2,1,0:T(8,128)S(1)}, f32[1,16,128]{2,1,0:T(8,128)S(1)}, u32[]{:S(2)}, u32[]{:S(2)}) collective-permute-start(f32[1,16,128]{2,1,0:T(8,128)S(1)} %get-tuple-element.48), channel_id=1, source_target_pairs={{16,0},{32,16},{48,32},{64,48},{80,64},{96,80},{112,96},{128,112},... | collective-permute-start | bytes 24584 | tf_op jit(solution)/shard_map/ppermute | solution.py:21
  379.5 1.9 collective-permute-start.29
  381.5 7.5 %collective-permute-start.32 = (f32[18,1,128]{2,1,0:T(1,128)S(1)}, f32[18,1,128]{2,1,0:T(1,128)S(1)}, u32[]{:S(2)}, u32[]{:S(2)}) collective-permute-start(f32[18,1,128]{2,1,0:T(1,128)S(1)} %get-tuple-element.36), channel_id=1, source_target_pairs={{1,0},{2,1},{3,2},{4,3},{5,4},{6,5},{7,6},{8,7},{9,8},{10,9},{11,1... | collective-permute-start | bytes 27656 | tf_op jit(solution)/shard_map/ppermute | solution.py:21
  393.0 5.1 %collective-permute-done.33 = f32[18,1,128]{2,1,0:T(1,128)S(1)} collective-permute-done((f32[18,1,128]{2,1,0:T(1,128)S(1)}, f32[18,1,128]{2,1,0:T(1,128)S(1)}, u32[]{:S(2)}, u32[]{:S(2)}) %collective-permute-start.33) | collective-permute-done | bytes 9248 | tf_op jit(solution)/shard_map/ppermute | solution.py:19
  398.3 1.9 collective-permute-start.35
  400.2 5.8 %collective-permute-start.36 = (f32[1,16,128]{2,1,0:T(8,128)S(1)}, f32[1,16,128]{2,1,0:T(8,128)S(1)}, u32[]{:S(2)}, u32[]{:S(2)}) collective-permute-start(f32[1,16,128]{2,1,0:T(8,128)S(1)} %get-tuple-element.25), channel_id=1, source_target_pairs={{16,0},{32,16},{48,32},{64,48},{80,64},{96,80},{112,96},{128,112},... | collective-permute-start | bytes 24584 | tf_op jit(solution)/shard_map/ppermute | solution.py:21
  408.0 5.8 %collective-permute-start.39 = (f32[1,16,128]{2,1,0:T(8,128)S(1)}, f32[1,16,128]{2,1,0:T(8,128)S(1)}, u32[]{:S(2)}, u32[]{:S(2)}) collective-permute-start(f32[1,16,128]{2,1,0:T(8,128)S(1)} %get-tuple-element.46), channel_id=1, source_target_pairs={{16,0},{32,16},{48,32},{64,48},{80,64},{96,80},{112,96},{128,112},... | collective-permute-start | bytes 24584 | tf_op jit(solution)/shard_map/ppermute | solution.py:21
  413.8 1.9 collective-permute-start.37
  415.8 7.5 %collective-permute-start.40 = (f32[18,1,128]{2,1,0:T(1,128)S(1)}, f32[18,1,128]{2,1,0:T(1,128)S(1)}, u32[]{:S(2)}, u32[]{:S(2)}) collective-permute-start(f32[18,1,128]{2,1,0:T(1,128)S(1)} %get-tuple-element.34), channel_id=1, source_target_pairs={{1,0},{2,1},{3,2},{4,3},{5,4},{6,5},{7,6},{8,7},{9,8},{10,9},{11,1... | collective-permute-start | bytes 27656 | tf_op jit(solution)/shard_map/ppermute | solution.py:21
  427.4 5.1 %collective-permute-done.41 = f32[18,1,128]{2,1,0:T(1,128)S(1)} collective-permute-done((f32[18,1,128]{2,1,0:T(1,128)S(1)}, f32[18,1,128]{2,1,0:T(1,128)S(1)}, u32[]{:S(2)}, u32[]{:S(2)}) %collective-permute-start.41) | collective-permute-done | bytes 9248 | tf_op jit(solution)/shard_map/ppermute | solution.py:19
  434.6 5.8 %collective-permute-start.44 = (f32[1,16,128]{2,1,0:T(8,128)S(1)}, f32[1,16,128]{2,1,0:T(8,128)S(1)}, u32[]{:S(2)}, u32[]{:S(2)}) collective-permute-start(f32[1,16,128]{2,1,0:T(8,128)S(1)} %get-tuple-element.23), channel_id=1, source_target_pairs={{16,0},{32,16},{48,32},{64,48},{80,64},{96,80},{112,96},{128,112},... | collective-permute-start | bytes 24584 | tf_op jit(solution)/shard_map/ppermute | solution.py:21
  442.3 5.8 %collective-permute-start.47 = (f32[1,16,128]{2,1,0:T(8,128)S(1)}, f32[1,16,128]{2,1,0:T(8,128)S(1)}, u32[]{:S(2)}, u32[]{:S(2)}) collective-permute-start(f32[1,16,128]{2,1,0:T(8,128)S(1)} %get-tuple-element.45), channel_id=1, source_target_pairs={{16,0},{32,16},{48,32},{64,48},{80,64},{96,80},{112,96},{128,112},... | collective-permute-start | bytes 24584 | tf_op jit(solution)/shard_map/ppermute | solution.py:21
  450.1 7.5 %collective-permute-start.48 = (f32[18,1,128]{2,1,0:T(1,128)S(1)}, f32[18,1,128]{2,1,0:T(1,128)S(1)}, u32[]{:S(2)}, u32[]{:S(2)}) collective-permute-start(f32[18,1,128]{2,1,0:T(1,128)S(1)} %get-tuple-element.32), channel_id=1, source_target_pairs={{1,0},{2,1},{3,2},{4,3},{5,4},{6,5},{7,6},{8,7},{9,8},{10,9},{11,1... | collective-permute-start | bytes 27656 | tf_op jit(solution)/shard_map/ppermute | solution.py:21
  459.7 7.1 %collective-permute-done.49 = f32[18,1,128]{2,1,0:T(1,128)S(1)} collective-permute-done((f32[18,1,128]{2,1,0:T(1,128)S(1)}, f32[18,1,128]{2,1,0:T(1,128)S(1)}, u32[]{:S(2)}, u32[]{:S(2)}) %collective-permute-start.49) | collective-permute-done | bytes 9248 | tf_op jit(solution)/shard_map/ppermute | solution.py:19
  (168 shorter events, 43.7 us)
Async XLA Ops:
  9.3 32.5 %all-to-all-start = ((bf16[32,128,128]{2,1,0:T(8,128)(2,1)}), bf16[32,128,128]{2,1,0:T(8,128)(2,1)S(1)}, u32[]{:S(2)}, u32[]{:S(2)}) async-start(bf16[32,128,128]{2,1,0:T(8,128)(2,1)} %stack.2), calls=%async_computation | async-start | bytes 2097152 | tf_op jit(solution)/shard_map/all_to_all | solution.py:63
  17.6 254.6 %reduce-scatter.2.cloned.1.call-start = ((), (), s32[]{:S(2)}) async-start(), calls=%async_computation.2 | async-start | bytes 2228224 | tf_op jit(solution)/shard_map/reduce_scatter | solution.py:87
  59.0 222.0 %collective-permute-start.4 = (f32[1,16,128]{2,1,0:T(8,128)S(1)}, f32[1,16,128]{2,1,0:T(8,128)S(1)}, u32[]{:S(2)}, u32[]{:S(2)}) collective-permute-start(f32[1,16,128]{2,1,0:T(8,128)S(1)} %broadcast.94), channel_id=1, source_target_pairs={{0,16},{16,32},{32,48},{48,64},{64,80},{80,96},{96,112},{112,128},... | collective-permute-start | bytes 24584 | tf_op jit(solution)/shard_map/ppermute | solution.py:19
  61.5 219.5 %collective-permute-start.5 = (f32[1,16,128]{2,1,0:T(8,128)S(1)}, f32[1,16,128]{2,1,0:T(8,128)S(1)}, u32[]{:S(2)}, u32[]{:S(2)}) collective-permute-start(f32[1,16,128]{2,1,0:T(8,128)S(1)} %broadcast.94), channel_id=1, source_target_pairs={{16,0},{32,16},{48,32},{64,48},{80,64},{96,80},{112,96},{128,112},... | collective-permute-start | bytes 24584 | tf_op jit(solution)/shard_map/ppermute | solution.py:21
  75.8 9.5 %collective-permute-start.2 = (f32[18,1]{1,0:T(8,128)S(1)}, f32[18,1]{1,0:T(8,128)S(1)}, u32[]{:S(2)}, u32[]{:S(2)}) collective-permute-start(f32[18,1]{1,0:T(8,128)S(1)} %get-tuple-element.56), channel_id=1, source_target_pairs={{0,1},{1,2},{2,3},{3,4},{4,5},{5,6},{6,7},{7,8},{8,9},{9,10},{10,1... | collective-permute-start | bytes 224 | tf_op jit(solution)/shard_map/ppermute | solution.py:19
  273.3 10.2 %collective-permute-start.7 = (f32[1,16,128]{2,1,0:T(8,128)S(1)}, f32[1,16,128]{2,1,0:T(8,128)S(1)}, u32[]{:S(2)}, u32[]{:S(2)}) collective-permute-start(f32[1,16,128]{2,1,0:T(8,128)S(1)} %get-tuple-element.55), channel_id=1, source_target_pairs={{0,16},{16,32},{32,48},{48,64},{64,80},{80,96},{96,112},{112,128},... | collective-permute-start | bytes 24584 | tf_op jit(solution)/shard_map/ppermute | solution.py:19
  275.2 8.3 %collective-permute-start.8 = (f32[1,16,128]{2,1,0:T(8,128)S(1)}, f32[1,16,128]{2,1,0:T(8,128)S(1)}, u32[]{:S(2)}, u32[]{:S(2)}) collective-permute-start(f32[1,16,128]{2,1,0:T(8,128)S(1)} %get-tuple-element.54), channel_id=1, source_target_pairs={{16,0},{32,16},{48,32},{64,48},{80,64},{96,80},{112,96},{128,112},... | collective-permute-start | bytes 24584 | tf_op jit(solution)/shard_map/ppermute | solution.py:21
  281.1 14.1 %collective-permute-start.6 = (f32[18,1,128]{2,1,0:T(1,128)S(1)}, f32[18,1,128]{2,1,0:T(1,128)S(1)}, u32[]{:S(2)}, u32[]{:S(2)}) collective-permute-start(f32[18,1,128]{2,1,0:T(1,128)S(1)} %pad_maximum_fusion.83), channel_id=1, source_target_pairs={{0,1},{1,2},{2,3},{3,4},{4,5},{5,6},{6,7},{7,8},{8,9},{9,10},{10,1... | collective-permute-start | bytes 27656 | tf_op jit(solution)/shard_map/ppermute | solution.py:19
  283.6 11.6 %collective-permute-start.10 = (f32[18,1,128]{2,1,0:T(1,128)S(1)}, f32[18,1,128]{2,1,0:T(1,128)S(1)}, u32[]{:S(2)}, u32[]{:S(2)}) collective-permute-start(f32[18,1,128]{2,1,0:T(1,128)S(1)} %get-tuple-element.43), channel_id=1, source_target_pairs={{0,1},{1,2},{2,3},{3,4},{4,5},{5,6},{6,7},{7,8},{8,9},{9,10},{10,1... | collective-permute-start | bytes 27656 | tf_op jit(solution)/shard_map/ppermute | solution.py:19
  293.2 29.6 %collective-permute-start.18 = (f32[1,16,128]{2,1,0:T(8,128)S(1)}, f32[1,16,128]{2,1,0:T(8,128)S(1)}, u32[]{:S(2)}, u32[]{:S(2)}) collective-permute-start(f32[1,16,128]{2,1,0:T(8,128)S(1)} %slice.550), channel_id=1, source_target_pairs={{0,16},{16,32},{32,48},{48,64},{64,80},{80,96},{96,112},{112,128},... | collective-permute-start | bytes 24584 | tf_op jit(solution)/shard_map/ppermute | solution.py:19
  295.3 15.5 %collective-permute-start.11 = (f32[1,16,128]{2,1,0:T(8,128)S(1)}, f32[1,16,128]{2,1,0:T(8,128)S(1)}, u32[]{:S(2)}, u32[]{:S(2)}) collective-permute-start(f32[1,16,128]{2,1,0:T(8,128)S(1)} %get-tuple-element.30), channel_id=1, source_target_pairs={{0,16},{16,32},{32,48},{48,64},{64,80},{80,96},{96,112},{112,128},... | collective-permute-start | bytes 24584 | tf_op jit(solution)/shard_map/ppermute | solution.py:19
  297.2 13.6 %collective-permute-start.12 = (f32[1,16,128]{2,1,0:T(8,128)S(1)}, f32[1,16,128]{2,1,0:T(8,128)S(1)}, u32[]{:S(2)}, u32[]{:S(2)}) collective-permute-start(f32[1,16,128]{2,1,0:T(8,128)S(1)} %get-tuple-element.31), channel_id=1, source_target_pairs={{16,0},{32,16},{48,32},{64,48},{80,64},{96,80},{112,96},{128,112},... | collective-permute-start | bytes 24584 | tf_op jit(solution)/shard_map/ppermute | solution.py:21
  303.1 12.2 %collective-permute-start.14 = (f32[1,16,128]{2,1,0:T(8,128)S(1)}, f32[1,16,128]{2,1,0:T(8,128)S(1)}, u32[]{:S(2)}, u32[]{:S(2)}) collective-permute-start(f32[1,16,128]{2,1,0:T(8,128)S(1)} %get-tuple-element.53), channel_id=1, source_target_pairs={{0,16},{16,32},{32,48},{48,64},{64,80},{80,96},{96,112},{112,128},... | collective-permute-start | bytes 24584 | tf_op jit(solution)/shard_map/ppermute | solution.py:19
  305.1 10.3 %collective-permute-start.15 = (f32[1,16,128]{2,1,0:T(8,128)S(1)}, f32[1,16,128]{2,1,0:T(8,128)S(1)}, u32[]{:S(2)}, u32[]{:S(2)}) collective-permute-start(f32[1,16,128]{2,1,0:T(8,128)S(1)} %get-tuple-element.52), channel_id=1, source_target_pairs={{16,0},{32,16},{48,32},{64,48},{80,64},{96,80},{112,96},{128,112},... | collective-permute-start | bytes 24584 | tf_op jit(solution)/shard_map/ppermute | solution.py:21
  310.9 14.0 %collective-permute-start.13 = (f32[18,1,128]{2,1,0:T(1,128)S(1)}, f32[18,1,128]{2,1,0:T(1,128)S(1)}, u32[]{:S(2)}, u32[]{:S(2)}) collective-permute-start(f32[18,1,128]{2,1,0:T(1,128)S(1)} %pad_maximum_fusion.78), channel_id=1, source_target_pairs={{0,1},{1,2},{2,3},{3,4},{4,5},{5,6},{6,7},{7,8},{8,9},{9,10},{10,1... | collective-permute-start | bytes 27656 | tf_op jit(solution)/shard_map/ppermute | solution.py:19
  315.4 9.5 %collective-permute-start.16 = (f32[18,1,128]{2,1,0:T(1,128)S(1)}, f32[18,1,128]{2,1,0:T(1,128)S(1)}, u32[]{:S(2)}, u32[]{:S(2)}) collective-permute-start(f32[18,1,128]{2,1,0:T(1,128)S(1)} %get-tuple-element.40), channel_id=1, source_target_pairs={{1,0},{2,1},{3,2},{4,3},{5,4},{6,5},{7,6},{8,7},{9,8},{10,9},{11,1... | collective-permute-start | bytes 27656 | tf_op jit(solution)/shard_map/ppermute | solution.py:21
  320.4 9.2 %collective-permute-start.17 = (f32[18,1,128]{2,1,0:T(1,128)S(1)}, f32[18,1,128]{2,1,0:T(1,128)S(1)}, u32[]{:S(2)}, u32[]{:S(2)}) collective-permute-start(f32[18,1,128]{2,1,0:T(1,128)S(1)} %get-tuple-element.41), channel_id=1, source_target_pairs={{0,1},{1,2},{2,3},{3,4},{4,5},{5,6},{6,7},{7,8},{8,9},{9,10},{10,1... | collective-permute-start | bytes 27656 | tf_op jit(solution)/shard_map/ppermute | solution.py:19
  322.9 33.7 %collective-permute-start.26 = (f32[1,16,128]{2,1,0:T(8,128)S(1)}, f32[1,16,128]{2,1,0:T(8,128)S(1)}, u32[]{:S(2)}, u32[]{:S(2)}) collective-permute-start(f32[1,16,128]{2,1,0:T(8,128)S(1)} %slice.561), channel_id=1, source_target_pairs={{0,16},{16,32},{32,48},{48,64},{64,80},{80,96},{96,112},{112,128},... | collective-permute-start | bytes 24584 | tf_op jit(solution)/shard_map/ppermute | solution.py:19
  329.7 15.5 %collective-permute-start.19 = (f32[1,16,128]{2,1,0:T(8,128)S(1)}, f32[1,16,128]{2,1,0:T(8,128)S(1)}, u32[]{:S(2)}, u32[]{:S(2)}) collective-permute-start(f32[1,16,128]{2,1,0:T(8,128)S(1)} %get-tuple-element.28), channel_id=1, source_target_pairs={{0,16},{16,32},{32,48},{48,64},{64,80},{80,96},{96,112},{112,128},... | collective-permute-start | bytes 24584 | tf_op jit(solution)/shard_map/ppermute | solution.py:19
  331.6 13.5 %collective-permute-start.20 = (f32[1,16,128]{2,1,0:T(8,128)S(1)}, f32[1,16,128]{2,1,0:T(8,128)S(1)}, u32[]{:S(2)}, u32[]{:S(2)}) collective-permute-start(f32[1,16,128]{2,1,0:T(8,128)S(1)} %get-tuple-element.29), channel_id=1, source_target_pairs={{16,0},{32,16},{48,32},{64,48},{80,64},{96,80},{112,96},{128,112},... | collective-permute-start | bytes 24584 | tf_op jit(solution)/shard_map/ppermute | solution.py:21
  337.4 9.7 %collective-permute-start.22 = (f32[1,16,128]{2,1,0:T(8,128)S(1)}, f32[1,16,128]{2,1,0:T(8,128)S(1)}, u32[]{:S(2)}, u32[]{:S(2)}) collective-permute-start(f32[1,16,128]{2,1,0:T(8,128)S(1)} %get-tuple-element.51), channel_id=1, source_target_pairs={{0,16},{16,32},{32,48},{48,64},{64,80},{80,96},{96,112},{112,128},... | collective-permute-start | bytes 24584 | tf_op jit(solution)/shard_map/ppermute | solution.py:19
  339.4 7.7 %collective-permute-start.23 = (f32[1,16,128]{2,1,0:T(8,128)S(1)}, f32[1,16,128]{2,1,0:T(8,128)S(1)}, u32[]{:S(2)}, u32[]{:S(2)}) collective-permute-start(f32[1,16,128]{2,1,0:T(8,128)S(1)} %get-tuple-element.50), channel_id=1, source_target_pairs={{16,0},{32,16},{48,32},{64,48},{80,64},{96,80},{112,96},{128,112},... | collective-permute-start | bytes 24584 | tf_op jit(solution)/shard_map/ppermute | solution.py:21
  345.2 13.5 %collective-permute-start.21 = (f32[18,1,128]{2,1,0:T(1,128)S(1)}, f32[18,1,128]{2,1,0:T(1,128)S(1)}, u32[]{:S(2)}, u32[]{:S(2)}) collective-permute-start(f32[18,1,128]{2,1,0:T(1,128)S(1)} %pad_maximum_fusion.73), channel_id=1, source_target_pairs={{0,1},{1,2},{2,3},{3,4},{4,5},{5,6},{6,7},{7,8},{8,9},{9,10},{10,1... | collective-permute-start | bytes 27656 | tf_op jit(solution)/shard_map/ppermute | solution.py:19
  347.1 11.6 %collective-permute-start.24 = (f32[18,1,128]{2,1,0:T(1,128)S(1)}, f32[18,1,128]{2,1,0:T(1,128)S(1)}, u32[]{:S(2)}, u32[]{:S(2)}) collective-permute-start(f32[18,1,128]{2,1,0:T(1,128)S(1)} %get-tuple-element.38), channel_id=1, source_target_pairs={{1,0},{2,1},{3,2},{4,3},{5,4},{6,5},{7,6},{8,7},{9,8},{10,9},{11,1... | collective-permute-start | bytes 27656 | tf_op jit(solution)/shard_map/ppermute | solution.py:21
  354.7 9.2 %collective-permute-start.25 = (f32[18,1,128]{2,1,0:T(1,128)S(1)}, f32[18,1,128]{2,1,0:T(1,128)S(1)}, u32[]{:S(2)}, u32[]{:S(2)}) collective-permute-start(f32[18,1,128]{2,1,0:T(1,128)S(1)} %get-tuple-element.39), channel_id=1, source_target_pairs={{0,1},{1,2},{2,3},{3,4},{4,5},{5,6},{6,7},{7,8},{8,9},{9,10},{10,1... | collective-permute-start | bytes 27656 | tf_op jit(solution)/shard_map/ppermute | solution.py:19
  356.8 34.2 %collective-permute-start.34 = (f32[1,16,128]{2,1,0:T(8,128)S(1)}, f32[1,16,128]{2,1,0:T(8,128)S(1)}, u32[]{:S(2)}, u32[]{:S(2)}) collective-permute-start(f32[1,16,128]{2,1,0:T(8,128)S(1)} %slice.572), channel_id=1, source_target_pairs={{0,16},{16,32},{32,48},{48,64},{64,80},{80,96},{96,112},{112,128},... | collective-permute-start | bytes 24584 | tf_op jit(solution)/shard_map/ppermute | solution.py:19
  364.0 15.5 %collective-permute-start.27 = (f32[1,16,128]{2,1,0:T(8,128)S(1)}, f32[1,16,128]{2,1,0:T(8,128)S(1)}, u32[]{:S(2)}, u32[]{:S(2)}) collective-permute-start(f32[1,16,128]{2,1,0:T(8,128)S(1)} %get-tuple-element.26), channel_id=1, source_target_pairs={{0,16},{16,32},{32,48},{48,64},{64,80},{80,96},{96,112},{112,128},... | collective-permute-start | bytes 24584 | tf_op jit(solution)/shard_map/ppermute | solution.py:19
  365.9 13.5 %collective-permute-start.28 = (f32[1,16,128]{2,1,0:T(8,128)S(1)}, f32[1,16,128]{2,1,0:T(8,128)S(1)}, u32[]{:S(2)}, u32[]{:S(2)}) collective-permute-start(f32[1,16,128]{2,1,0:T(8,128)S(1)} %get-tuple-element.27), channel_id=1, source_target_pairs={{16,0},{32,16},{48,32},{64,48},{80,64},{96,80},{112,96},{128,112},... | collective-permute-start | bytes 24584 | tf_op jit(solution)/shard_map/ppermute | solution.py:21
  371.8 9.7 %collective-permute-start.30 = (f32[1,16,128]{2,1,0:T(8,128)S(1)}, f32[1,16,128]{2,1,0:T(8,128)S(1)}, u32[]{:S(2)}, u32[]{:S(2)}) collective-permute-start(f32[1,16,128]{2,1,0:T(8,128)S(1)} %get-tuple-element.49), channel_id=1, source_target_pairs={{0,16},{16,32},{32,48},{48,64},{64,80},{80,96},{96,112},{112,128},... | collective-permute-start | bytes 24584 | tf_op jit(solution)/shard_map/ppermute | solution.py:19
  373.7 7.7 %collective-permute-start.31 = (f32[1,16,128]{2,1,0:T(8,128)S(1)}, f32[1,16,128]{2,1,0:T(8,128)S(1)}, u32[]{:S(2)}, u32[]{:S(2)}) collective-permute-start(f32[1,16,128]{2,1,0:T(8,128)S(1)} %get-tuple-element.48), channel_id=1, source_target_pairs={{16,0},{32,16},{48,32},{64,48},{80,64},{96,80},{112,96},{128,112},... | collective-permute-start | bytes 24584 | tf_op jit(solution)/shard_map/ppermute | solution.py:21
  379.5 13.5 %collective-permute-start.29 = (f32[18,1,128]{2,1,0:T(1,128)S(1)}, f32[18,1,128]{2,1,0:T(1,128)S(1)}, u32[]{:S(2)}, u32[]{:S(2)}) collective-permute-start(f32[18,1,128]{2,1,0:T(1,128)S(1)} %pad_maximum_fusion.68), channel_id=1, source_target_pairs={{0,1},{1,2},{2,3},{3,4},{4,5},{5,6},{6,7},{7,8},{8,9},{9,10},{10,1... | collective-permute-start | bytes 27656 | tf_op jit(solution)/shard_map/ppermute | solution.py:19
  381.5 11.6 %collective-permute-start.32 = (f32[18,1,128]{2,1,0:T(1,128)S(1)}, f32[18,1,128]{2,1,0:T(1,128)S(1)}, u32[]{:S(2)}, u32[]{:S(2)}) collective-permute-start(f32[18,1,128]{2,1,0:T(1,128)S(1)} %get-tuple-element.36), channel_id=1, source_target_pairs={{1,0},{2,1},{3,2},{4,3},{5,4},{6,5},{7,6},{8,7},{9,8},{10,9},{11,1... | collective-permute-start | bytes 27656 | tf_op jit(solution)/shard_map/ppermute | solution.py:21
  389.0 9.2 %collective-permute-start.33 = (f32[18,1,128]{2,1,0:T(1,128)S(1)}, f32[18,1,128]{2,1,0:T(1,128)S(1)}, u32[]{:S(2)}, u32[]{:S(2)}) collective-permute-start(f32[18,1,128]{2,1,0:T(1,128)S(1)} %get-tuple-element.37), channel_id=1, source_target_pairs={{0,1},{1,2},{2,3},{3,4},{4,5},{5,6},{6,7},{7,8},{8,9},{9,10},{10,1... | collective-permute-start | bytes 27656 | tf_op jit(solution)/shard_map/ppermute | solution.py:19
  391.1 34.2 %collective-permute-start.42 = (f32[1,16,128]{2,1,0:T(8,128)S(1)}, f32[1,16,128]{2,1,0:T(8,128)S(1)}, u32[]{:S(2)}, u32[]{:S(2)}) collective-permute-start(f32[1,16,128]{2,1,0:T(8,128)S(1)} %slice.583), channel_id=1, source_target_pairs={{0,16},{16,32},{32,48},{48,64},{64,80},{80,96},{96,112},{112,128},... | collective-permute-start | bytes 24584 | tf_op jit(solution)/shard_map/ppermute | solution.py:19
  398.3 15.5 %collective-permute-start.35 = (f32[1,16,128]{2,1,0:T(8,128)S(1)}, f32[1,16,128]{2,1,0:T(8,128)S(1)}, u32[]{:S(2)}, u32[]{:S(2)}) collective-permute-start(f32[1,16,128]{2,1,0:T(8,128)S(1)} %get-tuple-element.24), channel_id=1, source_target_pairs={{0,16},{16,32},{32,48},{48,64},{64,80},{80,96},{96,112},{112,128},... | collective-permute-start | bytes 24584 | tf_op jit(solution)/shard_map/ppermute | solution.py:19
  400.2 13.5 %collective-permute-start.36 = (f32[1,16,128]{2,1,0:T(8,128)S(1)}, f32[1,16,128]{2,1,0:T(8,128)S(1)}, u32[]{:S(2)}, u32[]{:S(2)}) collective-permute-start(f32[1,16,128]{2,1,0:T(8,128)S(1)} %get-tuple-element.25), channel_id=1, source_target_pairs={{16,0},{32,16},{48,32},{64,48},{80,64},{96,80},{112,96},{128,112},... | collective-permute-start | bytes 24584 | tf_op jit(solution)/shard_map/ppermute | solution.py:21
  406.1 9.7 %collective-permute-start.38 = (f32[1,16,128]{2,1,0:T(8,128)S(1)}, f32[1,16,128]{2,1,0:T(8,128)S(1)}, u32[]{:S(2)}, u32[]{:S(2)}) collective-permute-start(f32[1,16,128]{2,1,0:T(8,128)S(1)} %get-tuple-element.47), channel_id=1, source_target_pairs={{0,16},{16,32},{32,48},{48,64},{64,80},{80,96},{96,112},{112,128},... | collective-permute-start | bytes 24584 | tf_op jit(solution)/shard_map/ppermute | solution.py:19
  408.0 7.7 %collective-permute-start.39 = (f32[1,16,128]{2,1,0:T(8,128)S(1)}, f32[1,16,128]{2,1,0:T(8,128)S(1)}, u32[]{:S(2)}, u32[]{:S(2)}) collective-permute-start(f32[1,16,128]{2,1,0:T(8,128)S(1)} %get-tuple-element.46), channel_id=1, source_target_pairs={{16,0},{32,16},{48,32},{64,48},{80,64},{96,80},{112,96},{128,112},... | collective-permute-start | bytes 24584 | tf_op jit(solution)/shard_map/ppermute | solution.py:21
  413.8 13.5 %collective-permute-start.37 = (f32[18,1,128]{2,1,0:T(1,128)S(1)}, f32[18,1,128]{2,1,0:T(1,128)S(1)}, u32[]{:S(2)}, u32[]{:S(2)}) collective-permute-start(f32[18,1,128]{2,1,0:T(1,128)S(1)} %pad_maximum_fusion.63), channel_id=1, source_target_pairs={{0,1},{1,2},{2,3},{3,4},{4,5},{5,6},{6,7},{7,8},{8,9},{9,10},{10,1... | collective-permute-start | bytes 27656 | tf_op jit(solution)/shard_map/ppermute | solution.py:19
  415.8 11.6 %collective-permute-start.40 = (f32[18,1,128]{2,1,0:T(1,128)S(1)}, f32[18,1,128]{2,1,0:T(1,128)S(1)}, u32[]{:S(2)}, u32[]{:S(2)}) collective-permute-start(f32[18,1,128]{2,1,0:T(1,128)S(1)} %get-tuple-element.34), channel_id=1, source_target_pairs={{1,0},{2,1},{3,2},{4,3},{5,4},{6,5},{7,6},{8,7},{9,8},{10,9},{11,1... | collective-permute-start | bytes 27656 | tf_op jit(solution)/shard_map/ppermute | solution.py:21
  423.3 9.2 %collective-permute-start.41 = (f32[18,1,128]{2,1,0:T(1,128)S(1)}, f32[18,1,128]{2,1,0:T(1,128)S(1)}, u32[]{:S(2)}, u32[]{:S(2)}) collective-permute-start(f32[18,1,128]{2,1,0:T(1,128)S(1)} %get-tuple-element.35), channel_id=1, source_target_pairs={{0,1},{1,2},{2,3},{3,4},{4,5},{5,6},{6,7},{7,8},{8,9},{9,10},{10,1... | collective-permute-start | bytes 27656 | tf_op jit(solution)/shard_map/ppermute | solution.py:19
  425.4 34.2 %collective-permute-start.50 = (f32[1,16,128]{2,1,0:T(8,128)S(1)}, f32[1,16,128]{2,1,0:T(8,128)S(1)}, u32[]{:S(2)}, u32[]{:S(2)}) collective-permute-start(f32[1,16,128]{2,1,0:T(8,128)S(1)} %slice.594), channel_id=1, source_target_pairs={{0,16},{16,32},{32,48},{48,64},{64,80},{80,96},{96,112},{112,128},... | collective-permute-start | bytes 24584 | tf_op jit(solution)/shard_map/ppermute | solution.py:19
  432.6 15.5 %collective-permute-start.43 = (f32[1,16,128]{2,1,0:T(8,128)S(1)}, f32[1,16,128]{2,1,0:T(8,128)S(1)}, u32[]{:S(2)}, u32[]{:S(2)}) collective-permute-start(f32[1,16,128]{2,1,0:T(8,128)S(1)} %get-tuple-element.22), channel_id=1, source_target_pairs={{0,16},{16,32},{32,48},{48,64},{64,80},{80,96},{96,112},{112,128},... | collective-permute-start | bytes 24584 | tf_op jit(solution)/shard_map/ppermute | solution.py:19
  434.6 13.5 %collective-permute-start.44 = (f32[1,16,128]{2,1,0:T(8,128)S(1)}, f32[1,16,128]{2,1,0:T(8,128)S(1)}, u32[]{:S(2)}, u32[]{:S(2)}) collective-permute-start(f32[1,16,128]{2,1,0:T(8,128)S(1)} %get-tuple-element.23), channel_id=1, source_target_pairs={{16,0},{32,16},{48,32},{64,48},{80,64},{96,80},{112,96},{128,112},... | collective-permute-start | bytes 24584 | tf_op jit(solution)/shard_map/ppermute | solution.py:21
  440.4 9.7 %collective-permute-start.46 = (f32[1,16,128]{2,1,0:T(8,128)S(1)}, f32[1,16,128]{2,1,0:T(8,128)S(1)}, u32[]{:S(2)}, u32[]{:S(2)}) collective-permute-start(f32[1,16,128]{2,1,0:T(8,128)S(1)} %get-tuple-element.44), channel_id=1, source_target_pairs={{0,16},{16,32},{32,48},{48,64},{64,80},{80,96},{96,112},{112,128},... | collective-permute-start | bytes 24584 | tf_op jit(solution)/shard_map/ppermute | solution.py:19
  448.1 11.6 %collective-permute-start.45 = (f32[18,1,128]{2,1,0:T(1,128)S(1)}, f32[18,1,128]{2,1,0:T(1,128)S(1)}, u32[]{:S(2)}, u32[]{:S(2)}) collective-permute-start(f32[18,1,128]{2,1,0:T(1,128)S(1)} %pad_maximum_fusion.58), channel_id=1, source_target_pairs={{0,1},{1,2},{2,3},{3,4},{4,5},{5,6},{6,7},{7,8},{8,9},{9,10},{10,1... | collective-permute-start | bytes 27656 | tf_op jit(solution)/shard_map/ppermute | solution.py:19
  450.1 9.6 %collective-permute-start.48 = (f32[18,1,128]{2,1,0:T(1,128)S(1)}, f32[18,1,128]{2,1,0:T(1,128)S(1)}, u32[]{:S(2)}, u32[]{:S(2)}) collective-permute-start(f32[18,1,128]{2,1,0:T(1,128)S(1)} %get-tuple-element.32), channel_id=1, source_target_pairs={{1,0},{2,1},{3,2},{4,3},{5,4},{6,5},{7,6},{8,7},{9,8},{10,9},{11,1... | collective-permute-start | bytes 27656 | tf_op jit(solution)/shard_map/ppermute | solution.py:21
  457.7 9.2 %collective-permute-start.49 = (f32[18,1,128]{2,1,0:T(1,128)S(1)}, f32[18,1,128]{2,1,0:T(1,128)S(1)}, u32[]{:S(2)}, u32[]{:S(2)}) collective-permute-start(f32[18,1,128]{2,1,0:T(1,128)S(1)} %get-tuple-element.33), channel_id=1, source_target_pairs={{0,1},{1,2},{2,3},{3,4},{4,5},{5,6},{6,7},{7,8},{8,9},{9,10},{10,1... | collective-permute-start | bytes 27656 | tf_op jit(solution)/shard_map/ppermute | solution.py:19
  (19 other events, 220.1 us)
Sparse Core Ops, SparseCore 0:
  59.1 213.0 reduce-scatter.1
